TPU v7x, 32 devices: a whole 2x2x4 slice. The times are simulated.
32 devices in a mesh: img: 4 (over z), gx: 2 (over x), gz: 4 (over y, core).
Axes of the slice: x: 2, y: 2, z: 4, core: 2. Of those that a mesh axis runs over, the one named last changes fastest.
Arguments:
- species: float32 [4, 2, 32, 16, 512], P('img', None, 'gx', None, 'gz'), may hold values from -2.5 to 2.5
- diffusion: float32 [2, 32, 16, 512], P(None, 'gx', None, 'gz'), may hold values from 0.1 to 2
- z_inverse: float32 [2, 512, 512], replicated, may hold values from -1 to 1.5
- starts: int32 [4], replicated, may hold values from -1 to 1, as said below
- weights: float32 [4, 4], replicated, may hold values from -0.1 to 1, as said below
Outputs:
- new_string: float32 [4, 2, 32, 16, 512], P('img', None, 'gx', None, 'gz')
Inputs may be any that keep to these rules, and one draw needn't show every extreme that they name: starts[t] is t - 2 or t - 1. Each row holds the cubic Lagrange weights at a point between the second and third of four equally spaced images.
All inputs are finite; a program needn't handle non-finite values.
Results may differ from a plain program's by a relative error of at most 0.00012.
Values sent between devices are 32-bit elements; how exact they have to be, the bound alone decides.
A program may use at most 64 MiB of HBM per device.

v0:
```python
import jax
import jax.numpy as jnp
from jax import lax
from jax.sharding import PartitionSpec as P

STEPS = 4
step_size = 0.05


def with_halo(cells, sides, width):
    for axis, dim in sides:
        count = lax.axis_size(axis)
        ends = count - 1
        head = lax.slice_in_dim(cells, 0, width, axis=dim)
        tail = lax.slice_in_dim(cells, cells.shape[dim] - width, cells.shape[dim], axis=dim)
        cells = jnp.concatenate(
            [
                lax.ppermute(tail, axis, [(i, (i + 1) % count) for i in range(ends)]),
                cells,
                lax.ppermute(head, axis, [((i + 1) % count, i) for i in range(ends)]),
            ],
            axis=dim,
        )
    return cells


def passed_along(value, axis, steps):
    count = lax.axis_size(axis)
    first, last = (max(0, -steps), min(count, count - steps))
    return lax.ppermute(value, axis, [(source, source + steps) for source in range(first, last)])


def reaction(state):
    first = state[0]
    second = state[1]
    return jnp.stack([first - first * first * first - second + 0.2, 0.5 * (first - second)])


def spread_flux(state, padded, coeffs):
    centre = coeffs[:, 1:-1, 1:-1]
    total = (centre + coeffs[:, :-2, 1:-1]) * (padded[:, :-2, 1:-1] - state)
    total = total + (centre + coeffs[:, 2:, 1:-1]) * (padded[:, 2:, 1:-1] - state)
    total = total + (centre + coeffs[:, 1:-1, :-2]) * (padded[:, 1:-1, :-2] - state)
    total = total + (centre + coeffs[:, 1:-1, 2:]) * (padded[:, 1:-1, 2:] - state)
    return 0.5 * total


def local(species, diffusion, z_inverse, starts, weights):
    state = species[0]
    y_widths = ((0, 0), (0, 0), (1, 1), (0, 0))
    coeffs = with_halo(diffusion, (("gx", 1),), 1)
    coeffs = jnp.pad(coeffs, y_widths)
    for repeat in range(STEPS):
        padded = with_halo(state, (("gx", 1),), 1)
        padded = jnp.pad(padded, y_widths)
        source = state + step_size * (reaction(state) + spread_flux(state, padded, coeffs))
        solved = jnp.einsum(
            "sij,sabj->sabi",
            z_inverse,
            lax.all_to_all(source, "gz", split_axis=2, concat_axis=3, tiled=True),
            precision=lax.Precision.HIGHEST,
        )
        state = lax.all_to_all(solved, "gz", split_axis=3, concat_axis=2, tiled=True)
    before_one = passed_along(state, "img", 1)
    before_two = passed_along(state, "img", 2)
    after_one = passed_along(state, "img", -1)
    after_two = passed_along(state, "img", -2)
    images = lax.axis_size("img")
    target = lax.axis_index("img")
    listed = jnp.arange(images, dtype=jnp.int32)
    picked = listed == target
    first_image = jnp.sum(jnp.where(picked, starts, 0))
    my_weights = jnp.sum(jnp.where(picked[:, None], weights, 0.0), axis=0)
    sources = {-2: before_two, -1: before_one, 0: state, 1: after_one, 2: after_two}
    result = None
    for offset in range(-2, 3):
        coef = jnp.zeros((), jnp.float32)
        for place in range(4):
            coef = coef + jnp.where(first_image + place == target + offset, my_weights[place], 0.0)
        term = coef * sources[offset]
        result = term if result is None else result + term
    return result[None]


def solution(mesh):
    return jax.shard_map(
        local,
        mesh=mesh,
        in_specs=(P("img", None, "gx", None, "gz"), P(None, "gx", None, "gz"), P(), P(), P()),
        out_specs=P("img", None, "gx", None, "gz"),
        check_vma=False,
    )
```

profile of v0, /device:TPU:24, one launch (start us, length us, event | category | flops | bytes accessed | tf_op | source)
XLA Modules:
  0.0 201.2 jit_solution(16023715058296012637)
XLA Ops:
  0.0 0.9 fusion.80
  0.9 3.4 %collective-permute-start = (f32[2,1,16,128]{3,1,0,2:T(1,128)S(1)}, f32[2,1,16,128]{3,1,0,2:T(1,128)S(1)}, u32[]{:S(2)}, u32[]{:S(2)}) collective-permute-start(f32[2,1,16,128]{3,1,0,2:T(1,128)S(1)} %copy.23), channel_id=1, source_target_pairs={{0,4},{1,5},{2,6},{3,7},{8,12},{9,13},{10,14},{11,15},{16,20},{17,... | collective-permute-start | bytes 49160 | tf_op jit(solution)/shard_map/ppermute | solution.py:18
  4.4 1.3 collective-permute-start.2
  5.7 1.0 copy.70
  6.7 4.5 %collective-permute-start.1 = (f32[2,1,16,128]{3,1,0,2:T(1,128)S(1)}, f32[2,1,16,128]{3,1,0,2:T(1,128)S(1)}, u32[]{:S(2)}, u32[]{:S(2)}) collective-permute-start(f32[2,1,16,128]{3,1,0,2:T(1,128)S(1)} %get-tuple-element.32), channel_id=1, source_target_pairs={{0,4},{1,5},{2,6},{3,7},{8,12},{9,13},{10,14},{11,15},{16,20},{17,... | collective-permute-start | bytes 49160 | tf_op jit(solution)/shard_map/ppermute | solution.py:18
  11.3 1.3 collective-permute-start.3
  12.6 1.0 fusion.81
  13.7 1.0 copy.25
  14.7 2.2 %collective-permute-done.3 = f32[2,1,16,128]{3,1,0,2:T(1,128)S(1)} collective-permute-done((f32[2,1,16,128]{3,1,0,2:T(1,128)S(1)}, f32[2,1,16,128]{3,1,0,2:T(1,128)S(1)}, u32[]{:S(2)}, u32[]{:S(2)}) %collective-permute-start.3) | collective-permute-done | bytes 16416 | tf_op jit(solution)/shard_map/ppermute | solution.py:20
  17.5 8.6 %all_to_all.144 = f32[2,16,16,128]{3,1,0,2:T(8,128)S(1)} all-to-all(f32[2,16,16,128]{3,1,0,2:T(8,128)S(1)} %get-tuple-element.5), channel_id=1, replica_groups=mesh['img'=4,'gx'=2,'gz'=4] {'gz'}, dimensions={2} | all-to-all | bytes 524288 | tf_op jit(solution)/shard_map/all_to_all | solution.py:60
  26.1 0.9 copy.69
  27.0 1.1 all_to_all.107
  28.0 2.1 %fusion.6 = f32[2,16,4,512]{3,1,2,0:T(8,128)S(1)} fusion(f32[2,16,4,512]{3,1,2,0:T(8,128)S(1)} %all_to_all.107, f32[2,512,512]{2,1,0:T(8,128)S(1)} %copy-done), kind=kOutput, calls=%fused_computation.6 | convolution fusion | flops 402653184 | bytes 2621440 | tf_op jit(solution)/shard_map/sij,sabj->sabi/dot_general | solution.py:57
  30.2 1.7 copy.33
  31.9 3.1 %reshape.265 = f32[4,1,16384]{2,1,0:T(1,128)S(1)} reshape(f32[512,2,4,16]{3,2,1,0:T(4,128)} %bitcast.108) | data formatting | bytes 524288
  35.0 8.4 %all_to_all.145 = f32[4,1,16384]{2,1,0:T(1,128)S(1)} all-to-all(f32[4,1,16384]{2,1,0:T(1,128)S(1)} %reshape.265), channel_id=1, replica_groups=mesh['img'=4,'gx'=2,'gz'=4] {'gz'}, dimensions={0} | all-to-all | bytes 524288 | tf_op jit(solution)/shard_map/all_to_all | solution.py:63
  44.0 1.4 reduce
  45.4 2.9 %reshape.266 = f32[512,2,4,16]{3,2,1,0:T(4,128)} reshape(f32[4,16384]{1,0:T(4,128)S(1)} %reduce) | data formatting | bytes 524288
  48.3 1.8 copy.34
  50.1 2.4 %collective-permute-start.4 = (f32[2,1,16,128]{3,1,0,2:T(1,128)S(1)}, f32[2,1,16,128]{3,1,0,2:T(1,128)S(1)}, u32[]{:S(2)}, u32[]{:S(2)}) collective-permute-start(f32[2,1,16,128]{3,1,0,2:T(1,128)S(1)} %get-tuple-element.24), channel_id=1, source_target_pairs={{0,4},{1,5},{2,6},{3,7},{8,12},{9,13},{10,14},{11,15},{16,20},{17,... | collective-permute-start | bytes 49160 | tf_op jit(solution)/shard_map/ppermute | solution.py:18
  52.5 1.3 collective-permute-start.5
  53.9 4.2 %collective-permute-done.5 = f32[2,1,16,128]{3,1,0,2:T(1,128)S(1)} collective-permute-done((f32[2,1,16,128]{3,1,0,2:T(1,128)S(1)}, f32[2,1,16,128]{3,1,0,2:T(1,128)S(1)}, u32[]{:S(2)}, u32[]{:S(2)}) %collective-permute-start.5) | collective-permute-done | bytes 16416 | tf_op jit(solution)/shard_map/ppermute | solution.py:20
  58.5 8.4 %all_to_all.146 = f32[2,16,16,128]{3,1,0,2:T(8,128)S(1)} all-to-all(f32[2,16,16,128]{3,1,0,2:T(8,128)S(1)} %fusion.40), channel_id=1, replica_groups=mesh['img'=4,'gx'=2,'gz'=4] {'gz'}, dimensions={2} | all-to-all | bytes 524288 | tf_op jit(solution)/shard_map/all_to_all | solution.py:60
  67.0 0.9 copy.68
  67.8 1.1 all_to_all.115
  68.9 2.1 %fusion.4 = f32[2,16,4,512]{3,1,2,0:T(8,128)S(1)} fusion(f32[2,16,4,512]{3,1,2,0:T(8,128)S(1)} %all_to_all.115, f32[2,512,512]{2,1,0:T(8,128)S(1)} %copy-done), kind=kOutput, calls=%fused_computation.4 | convolution fusion | flops 402653184 | bytes 2621440 | tf_op jit(solution)/shard_map/sij,sabj->sabi/dot_general | solution.py:57
  71.0 1.7 copy.36
  72.8 3.1 %reshape.267 = f32[4,1,16384]{2,1,0:T(1,128)S(1)} reshape(f32[512,2,4,16]{3,2,1,0:T(4,128)} %bitcast.110) | data formatting | bytes 524288
  75.8 8.4 %all_to_all.147 = f32[4,1,16384]{2,1,0:T(1,128)S(1)} all-to-all(f32[4,1,16384]{2,1,0:T(1,128)S(1)} %reshape.267), channel_id=1, replica_groups=mesh['img'=4,'gx'=2,'gz'=4] {'gz'}, dimensions={0} | all-to-all | bytes 524288 | tf_op jit(solution)/shard_map/all_to_all | solution.py:63
  84.3 1.4 reduce.1
  85.7 2.9 %reshape.268 = f32[512,2,4,16]{3,2,1,0:T(4,128)} reshape(f32[4,16384]{1,0:T(4,128)S(1)} %reduce.1) | data formatting | bytes 524288
  88.5 1.8 copy.37
  90.4 1.6 collective-permute-start.6
  92.1 1.3 collective-permute-start.7
  93.5 4.2 %collective-permute-done.7 = f32[2,1,16,128]{3,1,0,2:T(1,128)S(1)} collective-permute-done((f32[2,1,16,128]{3,1,0,2:T(1,128)S(1)}, f32[2,1,16,128]{3,1,0,2:T(1,128)S(1)}, u32[]{:S(2)}, u32[]{:S(2)}) %collective-permute-start.7) | collective-permute-done | bytes 16416 | tf_op jit(solution)/shard_map/ppermute | solution.py:20
  98.1 8.4 %all_to_all.148 = f32[2,16,16,128]{3,1,0,2:T(8,128)S(1)} all-to-all(f32[2,16,16,128]{3,1,0,2:T(8,128)S(1)} %fusion.27), channel_id=1, replica_groups=mesh['img'=4,'gx'=2,'gz'=4] {'gz'}, dimensions={2} | all-to-all | bytes 524288 | tf_op jit(solution)/shard_map/all_to_all | solution.py:60
  106.5 0.9 copy.67
  107.4 1.1 all_to_all.123
  108.4 2.1 %fusion.2 = f32[2,16,4,512]{3,1,2,0:T(8,128)S(1)} fusion(f32[2,16,4,512]{3,1,2,0:T(8,128)S(1)} %all_to_all.123, f32[2,512,512]{2,1,0:T(8,128)S(1)} %copy-done), kind=kOutput, calls=%fused_computation.2 | convolution fusion | flops 402653184 | bytes 2621440 | tf_op jit(solution)/shard_map/sij,sabj->sabi/dot_general | solution.py:57
  110.6 1.7 copy.39
  112.3 3.1 %reshape.269 = f32[4,1,16384]{2,1,0:T(1,128)S(1)} reshape(f32[512,2,4,16]{3,2,1,0:T(4,128)} %bitcast.112) | data formatting | bytes 524288
  115.4 8.4 %all_to_all.149 = f32[4,1,16384]{2,1,0:T(1,128)S(1)} all-to-all(f32[4,1,16384]{2,1,0:T(1,128)S(1)} %reshape.269), channel_id=1, replica_groups=mesh['img'=4,'gx'=2,'gz'=4] {'gz'}, dimensions={0} | all-to-all | bytes 524288 | tf_op jit(solution)/shard_map/all_to_all | solution.py:63
  123.8 1.4 reduce.2
  125.2 2.9 %reshape.270 = f32[512,2,4,16]{3,2,1,0:T(4,128)} reshape(f32[4,16384]{1,0:T(4,128)S(1)} %reduce.2) | data formatting | bytes 524288
  128.1 1.8 copy.40
  130.0 1.6 collective-permute-start.8
  131.6 1.3 collective-permute-start.9
  133.1 4.2 %collective-permute-done.9 = f32[2,1,16,128]{3,1,0,2:T(1,128)S(1)} collective-permute-done((f32[2,1,16,128]{3,1,0,2:T(1,128)S(1)}, f32[2,1,16,128]{3,1,0,2:T(1,128)S(1)}, u32[]{:S(2)}, u32[]{:S(2)}) %collective-permute-start.9) | collective-permute-done | bytes 16416 | tf_op jit(solution)/shard_map/ppermute | solution.py:20
  137.6 8.4 %all_to_all.150 = f32[2,16,16,128]{3,1,0,2:T(8,128)S(1)} all-to-all(f32[2,16,16,128]{3,1,0,2:T(8,128)S(1)} %fusion.14), channel_id=1, replica_groups=mesh['img'=4,'gx'=2,'gz'=4] {'gz'}, dimensions={2} | all-to-all | bytes 524288 | tf_op jit(solution)/shard_map/all_to_all | solution.py:60
  146.3 2.1 %fusion = f32[2,16,4,512]{3,1,2,0:T(8,128)S(1)} fusion(f32[2,16,4,512]{3,1,2,0:T(8,128)S(1)} %all_to_all.131, f32[2,512,512]{2,1,0:T(8,128)S(1)} %copy-done), kind=kOutput, calls=%fused_computation | convolution fusion | flops 402653184 | bytes 2621440 | tf_op jit(solution)/shard_map/sij,sabj->sabi/dot_general | solution.py:57
  148.5 1.7 copy.42
  150.2 3.7 %reshape.271 = f32[4,1,16384]{2,1,0:T(1,128)} reshape(f32[512,2,4,16]{3,2,1,0:T(4,128)} %bitcast.114) | data formatting | bytes 524288
  153.9 3.4 %all-to-all-start.7 = ((f32[4,1,16384]{2,1,0:T(1,128)}), f32[4,1,16384]{2,1,0:T(1,128)S(1)}, u32[]{:S(2)}, u32[]{:S(2)}) async-start(f32[4,1,16384]{2,1,0:T(1,128)} %reshape.271), calls=%async_computation.7 | async-start | bytes 524288 | tf_op jit(solution)/shard_map/all_to_all | solution.py:63
  157.4 0.6 select_reduce_fusion.1
  158.0 5.4 %all-to-all-done.7 = f32[4,1,16384]{2,1,0:T(1,128)S(1)} async-done(((f32[4,1,16384]{2,1,0:T(1,128)}), f32[4,1,16384]{2,1,0:T(1,128)S(1)}, u32[]{:S(2)}, u32[]{:S(2)}) %all-to-all-start.7) | async-done | bytes 262176 | tf_op jit(solution)/shard_map/all_to_all | solution.py:63
  163.3 1.4 reduce.3
  164.8 2.9 %reshape.272 = f32[512,2,4,16]{3,2,1,0:T(4,128)} reshape(f32[4,16384]{1,0:T(4,128)S(1)} %reduce.3) | data formatting | bytes 524288
  167.6 1.9 copy.43
  169.5 1.3 collective-permute-start.10
  170.8 1.3 collective-permute-start.11
  172.1 4.6 %collective-permute-start.12 = (f32[2,16,16,128]{3,2,1,0:T(8,128)S(1)}, f32[2,16,16,128]{3,2,1,0:T(8,128)S(1)}, u32[]{:S(2)}, u32[]{:S(2)}) collective-permute-start(f32[2,16,16,128]{3,2,1,0:T(8,128)S(1)} %bitcast.133), channel_id=1, source_target_pairs={{8,0},{16,8},{24,16},{9,1},{17,9},{25,17},{10,2},{18,10},{26,18},{... | collective-permute-start | bytes 786440 | tf_op jit(solution)/shard_map/ppermute | solution.py:30
  176.7 5.5 %collective-permute-start.13 = (f32[2,16,16,128]{3,2,1,0:T(8,128)S(1)}, f32[2,16,16,128]{3,2,1,0:T(8,128)S(1)}, u32[]{:S(2)}, u32[]{:S(2)}) collective-permute-start(f32[2,16,16,128]{3,2,1,0:T(8,128)S(1)} %bitcast.134), channel_id=1, source_target_pairs={{16,0},{24,8},{17,1},{25,9},{18,2},{26,10},{19,3},{27,11},{20,4},{... | collective-permute-start | bytes 786440 | tf_op jit(solution)/shard_map/ppermute | solution.py:30
  186.8 0.7 fusion.83
  200.4 0.8 add_bitcast_fusion
  (45 shorter events, 3.3 us)
Async XLA Ops:
  0.0 28.0 %copy-start = (f32[2,512,512]{2,1,0:T(8,128)S(1)}, f32[2,512,512]{2,1,0:T(8,128)}, u32[]{:S(2)}) copy-start(f32[2,512,512]{2,1,0:T(8,128)} %param.7) | copy-start | bytes 6291460
  0.0 17.1 %copy-start.1 = (f32[2,16,16,128]{3,2,1,0:T(8,128)S(1)}, f32[2,16,16,128]{3,2,1,0:T(8,128)}, u32[]{:S(2)}) copy-start(f32[2,16,16,128]{3,2,1,0:T(8,128)} %param.6) | copy-start | bytes 786436
  0.9 16.1 %collective-permute-start = (f32[2,1,16,128]{3,1,0,2:T(1,128)S(1)}, f32[2,1,16,128]{3,1,0,2:T(1,128)S(1)}, u32[]{:S(2)}, u32[]{:S(2)}) collective-permute-start(f32[2,1,16,128]{3,1,0,2:T(1,128)S(1)} %copy.23), channel_id=1, source_target_pairs={{0,4},{1,5},{2,6},{3,7},{8,12},{9,13},{10,14},{11,15},{16,20},{17,... | collective-permute-start | bytes 49160 | tf_op jit(solution)/shard_map/ppermute | solution.py:18
  4.4 12.6 %collective-permute-start.2 = (f32[2,1,16,128]{3,1,0,2:T(1,128)S(1)}, f32[2,1,16,128]{3,1,0,2:T(1,128)S(1)}, u32[]{:S(2)}, u32[]{:S(2)}) collective-permute-start(f32[2,1,16,128]{3,1,0,2:T(1,128)S(1)} %copy.26), channel_id=1, source_target_pairs={{4,0},{5,1},{6,2},{7,3},{12,8},{13,9},{14,10},{15,11},{20,16},{21,... | collective-permute-start | bytes 49160 | tf_op jit(solution)/shard_map/ppermute | solution.py:20
  6.7 8.0 %collective-permute-start.1 = (f32[2,1,16,128]{3,1,0,2:T(1,128)S(1)}, f32[2,1,16,128]{3,1,0,2:T(1,128)S(1)}, u32[]{:S(2)}, u32[]{:S(2)}) collective-permute-start(f32[2,1,16,128]{3,1,0,2:T(1,128)S(1)} %get-tuple-element.32), channel_id=1, source_target_pairs={{0,4},{1,5},{2,6},{3,7},{8,12},{9,13},{10,14},{11,15},{16,20},{17,... | collective-permute-start | bytes 49160 | tf_op jit(solution)/shard_map/ppermute | solution.py:18
  11.3 5.6 %collective-permute-start.3 = (f32[2,1,16,128]{3,1,0,2:T(1,128)S(1)}, f32[2,1,16,128]{3,1,0,2:T(1,128)S(1)}, u32[]{:S(2)}, u32[]{:S(2)}) collective-permute-start(f32[2,1,16,128]{3,1,0,2:T(1,128)S(1)} %get-tuple-element.33), channel_id=1, source_target_pairs={{4,0},{5,1},{6,2},{7,3},{12,8},{13,9},{14,10},{15,11},{20,16},{21,... | collective-permute-start | bytes 49160 | tf_op jit(solution)/shard_map/ppermute | solution.py:20
  50.1 3.8 %collective-permute-start.4 = (f32[2,1,16,128]{3,1,0,2:T(1,128)S(1)}, f32[2,1,16,128]{3,1,0,2:T(1,128)S(1)}, u32[]{:S(2)}, u32[]{:S(2)}) collective-permute-start(f32[2,1,16,128]{3,1,0,2:T(1,128)S(1)} %get-tuple-element.24), channel_id=1, source_target_pairs={{0,4},{1,5},{2,6},{3,7},{8,12},{9,13},{10,14},{11,15},{16,20},{17,... | collective-permute-start | bytes 49160 | tf_op jit(solution)/shard_map/ppermute | solution.py:18
  52.5 5.6 %collective-permute-start.5 = (f32[2,1,16,128]{3,1,0,2:T(1,128)S(1)}, f32[2,1,16,128]{3,1,0,2:T(1,128)S(1)}, u32[]{:S(2)}, u32[]{:S(2)}) collective-permute-start(f32[2,1,16,128]{3,1,0,2:T(1,128)S(1)} %get-tuple-element.25), channel_id=1, source_target_pairs={{4,0},{5,1},{6,2},{7,3},{12,8},{13,9},{14,10},{15,11},{20,16},{21,... | collective-permute-start | bytes 49160 | tf_op jit(solution)/shard_map/ppermute | solution.py:20
  90.4 3.1 %collective-permute-start.6 = (f32[2,1,16,128]{3,1,0,2:T(1,128)S(1)}, f32[2,1,16,128]{3,1,0,2:T(1,128)S(1)}, u32[]{:S(2)}, u32[]{:S(2)}) collective-permute-start(f32[2,1,16,128]{3,1,0,2:T(1,128)S(1)} %get-tuple-element.18), channel_id=1, source_target_pairs={{0,4},{1,5},{2,6},{3,7},{8,12},{9,13},{10,14},{11,15},{16,20},{17,... | collective-permute-start | bytes 49160 | tf_op jit(solution)/shard_map/ppermute | solution.py:18
  92.1 5.6 %collective-permute-start.7 = (f32[2,1,16,128]{3,1,0,2:T(1,128)S(1)}, f32[2,1,16,128]{3,1,0,2:T(1,128)S(1)}, u32[]{:S(2)}, u32[]{:S(2)}) collective-permute-start(f32[2,1,16,128]{3,1,0,2:T(1,128)S(1)} %get-tuple-element.19), channel_id=1, source_target_pairs={{4,0},{5,1},{6,2},{7,3},{12,8},{13,9},{14,10},{15,11},{20,16},{21,... | collective-permute-start | bytes 49160 | tf_op jit(solution)/shard_map/ppermute | solution.py:20
  130.0 3.1 %collective-permute-start.8 = (f32[2,1,16,128]{3,1,0,2:T(1,128)S(1)}, f32[2,1,16,128]{3,1,0,2:T(1,128)S(1)}, u32[]{:S(2)}, u32[]{:S(2)}) collective-permute-start(f32[2,1,16,128]{3,1,0,2:T(1,128)S(1)} %get-tuple-element.12), channel_id=1, source_target_pairs={{0,4},{1,5},{2,6},{3,7},{8,12},{9,13},{10,14},{11,15},{16,20},{17,... | collective-permute-start | bytes 49160 | tf_op jit(solution)/shard_map/ppermute | solution.py:18
  131.6 5.6 %collective-permute-start.9 = (f32[2,1,16,128]{3,1,0,2:T(1,128)S(1)}, f32[2,1,16,128]{3,1,0,2:T(1,128)S(1)}, u32[]{:S(2)}, u32[]{:S(2)}) collective-permute-start(f32[2,1,16,128]{3,1,0,2:T(1,128)S(1)} %get-tuple-element.13), channel_id=1, source_target_pairs={{4,0},{5,1},{6,2},{7,3},{12,8},{13,9},{14,10},{15,11},{20,16},{21,... | collective-permute-start | bytes 49160 | tf_op jit(solution)/shard_map/ppermute | solution.py:20
  148.5 8.9 %copy-start.3 = (s32[4]{0:T(128)S(1)}, s32[4]{0:T(128)}, u32[]{:S(2)}) copy-start(s32[4]{0:T(128)} %param.8) | copy-start | bytes 52
  153.9 9.4 %all-to-all-start.7 = ((f32[4,1,16384]{2,1,0:T(1,128)}), f32[4,1,16384]{2,1,0:T(1,128)S(1)}, u32[]{:S(2)}, u32[]{:S(2)}) async-start(f32[4,1,16384]{2,1,0:T(1,128)} %reshape.271), calls=%async_computation.7 | async-start | bytes 524288 | tf_op jit(solution)/shard_map/all_to_all | solution.py:63
  164.8 22.0 %copy-start.2 = (f32[4,4]{1,0:T(4,128)S(1)}, f32[4,4]{1,0:T(4,128)}, u32[]{:S(2)}) copy-start(f32[4,4]{1,0:T(4,128)} %param.9) | copy-start | bytes 196
  169.5 30.8 %collective-permute-start.10 = (f32[2,16,16,128]{3,2,1,0:T(8,128)S(1)}, f32[2,16,16,128]{3,2,1,0:T(8,128)S(1)}, u32[]{:S(2)}, u32[]{:S(2)}) collective-permute-start(f32[2,16,16,128]{3,2,1,0:T(8,128)S(1)} %bitcast.131), channel_id=1, source_target_pairs={{0,16},{8,24},{1,17},{9,25},{2,18},{10,26},{3,19},{11,27},{4,20},{... | collective-permute-start | bytes 786440 | tf_op jit(solution)/shard_map/ppermute | solution.py:30
  170.8 29.5 %collective-permute-start.11 = (f32[2,16,16,128]{3,2,1,0:T(8,128)S(1)}, f32[2,16,16,128]{3,2,1,0:T(8,128)S(1)}, u32[]{:S(2)}, u32[]{:S(2)}) collective-permute-start(f32[2,16,16,128]{3,2,1,0:T(8,128)S(1)} %bitcast.132), channel_id=1, source_target_pairs={{0,8},{8,16},{16,24},{1,9},{9,17},{17,25},{2,10},{10,18},{18,26},{... | collective-permute-start | bytes 786440 | tf_op jit(solution)/shard_map/ppermute | solution.py:30
  172.1 28.2 %collective-permute-start.12 = (f32[2,16,16,128]{3,2,1,0:T(8,128)S(1)}, f32[2,16,16,128]{3,2,1,0:T(8,128)S(1)}, u32[]{:S(2)}, u32[]{:S(2)}) collective-permute-start(f32[2,16,16,128]{3,2,1,0:T(8,128)S(1)} %bitcast.133), channel_id=1, source_target_pairs={{8,0},{16,8},{24,16},{9,1},{17,9},{25,17},{10,2},{18,10},{26,18},{... | collective-permute-start | bytes 786440 | tf_op jit(solution)/shard_map/ppermute | solution.py:30
  176.7 23.7 %collective-permute-start.13 = (f32[2,16,16,128]{3,2,1,0:T(8,128)S(1)}, f32[2,16,16,128]{3,2,1,0:T(8,128)S(1)}, u32[]{:S(2)}, u32[]{:S(2)}) collective-permute-start(f32[2,16,16,128]{3,2,1,0:T(8,128)S(1)} %bitcast.134), channel_id=1, source_target_pairs={{16,0},{24,8},{17,1},{25,9},{18,2},{26,10},{19,3},{27,11},{20,4},{... | collective-permute-start | bytes 786440 | tf_op jit(solution)/shard_map/ppermute | solution.py:30
where the time goes:
time: 203 us; the launch traced here: 201 us
  blocking collectives  59.2 us (29%)
  local copies, waits for them, and re-layouts  50.2 us (25%)
  starting transfers between devices  36.1 us (18%)
  waiting for transfers between devices  20.4 us (10%)
  between operations  17.8 us (9%)
  other arithmetic  8.99 us (4%)
  matrix products  8.52 us (4%)
    all_to_all x4, blocking collectives, local(): lax.all_to_all(source, 'gz', split_axis=2, concat_axis=3, tiled=True)  33.9 us
    unnamed x18, local copies, waits for them, and re-layouts  26.4 us
    all_to_all x3, blocking collectives, local(): lax.all_to_all(solved, 'gz', split_axis=3, concat_axis=2, tiled=True)  25.3 us
    ppermute x5, waiting for transfers between devices, with_halo(): lax.ppermute(head, axis, [((i + 1) % count, i) for i in range(ends)])  14.8 us
    ppermute x5, starting transfers between devices, with_halo(): lax.ppermute(tail, axis, [(i, (i + 1) % count) for i in range(ends)])  13.6 us
    ppermute x4, starting transfers between devices, passed_along(): lax.ppermute(value, axis, [(source, source + steps) for source in range(f...  12.6 us
    dot_general x4, matrix products, local(): jnp.einsum('sij,sabj->sabi', z_inverse, lax.all_to_all(source, 'gz', spli...  8.52 us
    all_to_all x5, local copies, waits for them, and re-layouts, local(): lax.all_to_all(solved, 'gz', split_axis=3, concat_axis=2, tiled=True)  7.99 us
  transfers between devices with their start and end apart: 15, of which 8 were waited for; matrix products, arithmetic and copies ran while one was open for 2% of the time, Pallas kernels for 0%

commit v1 on v0

--- a/solution.py
+++ b/solution.py
@@ -60,7 +60,20 @@
             lax.all_to_all(source, "gz", split_axis=2, concat_axis=3, tiled=True),
             precision=lax.Precision.HIGHEST,
         )
-        state = lax.all_to_all(solved, "gz", split_axis=3, concat_axis=2, tiled=True)
+        block_now, top = (lax.axis_size("gz"), lax.axis_index("gz"))
+        block_next = solved.shape[3] // block_now
+        block_last = list(solved.shape)
+        block_last[3] = block_next
+        near = block_last[2]
+        block_last[2] = near * block_now
+        state = jnp.zeros(block_last, solved.dtype)
+        for no in range(block_now):
+            plain = lax.dynamic_slice_in_dim(solved, (top ^ no) * block_next, block_next, axis=3)
+            if no:
+                plain = lax.ppermute(
+                    plain, "gz", tuple(((dev_i, dev_i ^ no) for dev_i in range(block_now)))
+                )
+            state = lax.dynamic_update_slice_in_dim(state, plain, (top ^ no) * near, axis=2)
     before_one = passed_along(state, "img", 1)
     before_two = passed_along(state, "img", 2)
     after_one = passed_along(state, "img", -1)

time: 203 us -> 143 us (0.70)
  local copies, waits for them, and re-layouts: 50.2 us -> 7.14 us
  blocking collectives: 59.2 us -> 16.8 us
  waiting for transfers between devices: 20.4 us -> 40.2 us
  starting transfers between devices: 36.1 us -> 47.4 us
  other arithmetic: 8.99 us -> 4.14 us
    all_to_all x3 -> x0, blocking collectives: 25.3 us -> none  [local(): lax.all_to_all(solved, 'gz', split_axis=3, concat_axis=2, tiled=True)]
    unnamed x18 -> x10, local copies, waits for them, and re-layouts: 26.4 us -> 2.1 us
    all_to_all x4 -> x2, blocking collectives: 33.9 us -> 16.8 us  [local(): lax.all_to_all(source, 'gz', split_axis=2, concat_axis=3, tiled=True)]
    ppermute x0 -> x12, waiting for transfers between devices: none -> 14 us  [local(): lax.ppermute(plain, 'gz', tuple(((dev_i, dev_i ^ no) for dev_i in range(b...]
    all_to_all x5 -> x0, local copies, waits for them, and re-layouts: 7.99 us -> none  [local(): lax.all_to_all(solved, 'gz', split_axis=3, concat_axis=2, tiled=True)]
    ppermute x0 -> x12, starting transfers between devices: none -> 7.73 us  [local(): lax.ppermute(plain, 'gz', tuple(((dev_i, dev_i ^ no) for dev_i in range(b...]
    dot_general x4 -> x0, local copies, waits for them, and re-layouts: 6.95 us -> none  [local(): jnp.einsum('sij,sabj->sabi', z_inverse, lax.all_to_all(source, 'gz', spli...]
    all_to_all x1 -> x2, waiting for transfers between devices: 5.36 us -> 11.1 us  [local(): lax.all_to_all(source, 'gz', split_axis=2, concat_axis=3, tiled=True)]
  transfers between devices with their start and end apart: 15 -> 28, of which waited for: 8 -> 17; matrix products, arithmetic and copies ran while one was open for 2% -> 3% of each run, Pallas kernels for 0% -> 0%
where the time goes in v1:
time: 143 us; the launch traced here: 142 us
  starting transfers between devices  47.4 us (33%)
  waiting for transfers between devices  40.2 us (28%)
  between operations  18.1 us (13%)
  blocking collectives  16.8 us (12%)
  matrix products  8.52 us (6%)
  local copies, waits for them, and re-layouts  7.14 us (5%)
  other arithmetic  4.14 us (3%)
    all_to_all x2, blocking collectives, local(): lax.all_to_all(source, 'gz', split_axis=2, concat_axis=3, tiled=True)  16.8 us
    ppermute x5, waiting for transfers between devices, with_halo(): lax.ppermute(head, axis, [((i + 1) % count, i) for i in range(ends)])  14.8 us
    ppermute x12, waiting for transfers between devices, local(): lax.ppermute(plain, 'gz', tuple(((dev_i, dev_i ^ no) for dev_i in range(b...  14 us
    ppermute x5, starting transfers between devices, with_halo(): lax.ppermute(tail, axis, [(i, (i + 1) % count) for i in range(ends)])  13.6 us
    ppermute x4, starting transfers between devices, passed_along(): lax.ppermute(value, axis, [(source, source + steps) for source in range(f...  12.6 us
    all_to_all x2, waiting for transfers between devices, local(): lax.all_to_all(source, 'gz', split_axis=2, concat_axis=3, tiled=True)  11.1 us
    dot_general x4, matrix products, local(): jnp.einsum('sij,sabj->sabi', z_inverse, lax.all_to_all(source, 'gz', spli...  8.52 us
    ppermute x12, starting transfers between devices, local(): lax.ppermute(plain, 'gz', tuple(((dev_i, dev_i ^ no) for dev_i in range(b...  7.73 us
  transfers between devices with their start and end apart: 28, of which 17 were waited for; matrix products, arithmetic and copies ran while one was open for 3% of the time, Pallas kernels for 0%

profile of v1, /device:TPU:24, one launch (start us, length us, event | category | flops | bytes accessed | tf_op | source)
XLA Modules:
  0.0 142.3 jit_solution(11270501871440233423)
XLA Ops:
  0.0 0.9 fusion.74
  0.9 3.4 %collective-permute-start = (f32[2,1,16,128]{3,1,0,2:T(1,128)S(1)}, f32[2,1,16,128]{3,1,0,2:T(1,128)S(1)}, u32[]{:S(2)}, u32[]{:S(2)}) collective-permute-start(f32[2,1,16,128]{3,1,0,2:T(1,128)S(1)} %copy.29), channel_id=1, source_target_pairs={{0,4},{1,5},{2,6},{3,7},{8,12},{9,13},{10,14},{11,15},{16,20},{17,... | collective-permute-start | bytes 49160 | tf_op jit(solution)/shard_map/ppermute | solution.py:18
  4.4 1.3 collective-permute-start.2
  5.7 1.0 copy.101
  6.7 4.5 %collective-permute-start.1 = (f32[2,1,16,128]{3,1,0,2:T(1,128)S(1)}, f32[2,1,16,128]{3,1,0,2:T(1,128)S(1)}, u32[]{:S(2)}, u32[]{:S(2)}) collective-permute-start(f32[2,1,16,128]{3,1,0,2:T(1,128)S(1)} %get-tuple-element.42), channel_id=1, source_target_pairs={{0,4},{1,5},{2,6},{3,7},{8,12},{9,13},{10,14},{11,15},{16,20},{17,... | collective-permute-start | bytes 49160 | tf_op jit(solution)/shard_map/ppermute | solution.py:18
  11.3 1.3 collective-permute-start.3
  12.6 1.0 fusion.75
  13.7 1.0 copy.31
  14.7 2.2 %collective-permute-done.3 = f32[2,1,16,128]{3,1,0,2:T(1,128)S(1)} collective-permute-done((f32[2,1,16,128]{3,1,0,2:T(1,128)S(1)}, f32[2,1,16,128]{3,1,0,2:T(1,128)S(1)}, u32[]{:S(2)}, u32[]{:S(2)}) %collective-permute-start.3) | collective-permute-done | bytes 16416 | tf_op jit(solution)/shard_map/ppermute | solution.py:20
  17.1 1.1 fusion.53
  18.2 3.4 %all-to-all-start = ((f32[2,16,16,128]{3,1,0,2:T(8,128)}), f32[2,16,16,128]{3,1,0,2:T(8,128)S(1)}, u32[]{:S(2)}, u32[]{:S(2)}) async-start(f32[2,16,16,128]{3,1,0,2:T(8,128)} %get-tuple-element.5), calls=%async_computation | async-start | bytes 524288 | tf_op jit(solution)/shard_map/all_to_all | solution.py:60
  21.6 6.0 %all-to-all-done = f32[2,16,16,128]{3,1,0,2:T(8,128)S(1)} async-done(((f32[2,16,16,128]{3,1,0,2:T(8,128)}), f32[2,16,16,128]{3,1,0,2:T(8,128)S(1)}, u32[]{:S(2)}, u32[]{:S(2)}) %all-to-all-start) | async-done | bytes 262176 | tf_op jit(solution)/shard_map/all_to_all | solution.py:60
  27.6 0.2 copy.100
  27.7 0.1 all_to_all.55
  27.9 2.1 %fusion.6 = f32[2,16,4,512]{3,1,2,0:T(8,128)S(1)} fusion(f32[2,16,4,512]{3,1,2,0:T(8,128)S(1)} %all_to_all.55, f32[2,512,512]{2,1,0:T(8,128)S(1)} %copy-done), kind=kOutput, calls=%fused_computation.6 | convolution fusion | flops 402653184 | bytes 2621440 | tf_op jit(solution)/shard_map/sij,sabj->sabi/dot_general | solution.py:57
  30.1 0.4 collective-permute-start.5
  30.6 1.4 %collective-permute-start.6 = (f32[2,16,4,128]{3,1,2,0:T(8,128)S(1)}, f32[2,16,4,128]{3,1,2,0:T(8,128)S(1)}, u32[]{:S(2)}, u32[]{:S(2)}) collective-permute-start(f32[2,16,4,128]{3,1,2,0:T(8,128)S(1)} %get-tuple-element.32), channel_id=1, source_target_pairs={{0,3},{1,2},{2,1},{3,0},{4,7},{5,6},{6,5},{7,4},{8,11},{9,10},{10,... | collective-permute-start | bytes 196616 | tf_op jit(solution)/shard_map/ppermute | solution.py:73
  32.1 3.0 %collective-permute-done.5 = f32[2,16,4,128]{3,1,2,0:T(8,128)S(1)} collective-permute-done((f32[2,16,4,128]{3,1,2,0:T(8,128)S(1)}, f32[2,16,4,128]{3,1,2,0:T(8,128)S(1)}, u32[]{:S(2)}, u32[]{:S(2)}) %collective-permute-start.5) | collective-permute-done | bytes 65568 | tf_op jit(solution)/shard_map/ppermute | solution.py:73
  35.1 0.5 collective-permute-done.6
  35.6 2.4 %collective-permute-start.7 = (f32[2,1,16,128]{3,1,0,2:T(1,128)S(1)}, f32[2,1,16,128]{3,1,0,2:T(1,128)S(1)}, u32[]{:S(2)}, u32[]{:S(2)}) collective-permute-start(f32[2,1,16,128]{3,1,0,2:T(1,128)S(1)} %get-tuple-element.30), channel_id=1, source_target_pairs={{0,4},{1,5},{2,6},{3,7},{8,12},{9,13},{10,14},{11,15},{16,20},{17,... | collective-permute-start | bytes 49160 | tf_op jit(solution)/shard_map/ppermute | solution.py:18
  38.0 1.3 collective-permute-start.8
  39.4 4.2 %collective-permute-done.8 = f32[2,1,16,128]{3,1,0,2:T(1,128)S(1)} collective-permute-done((f32[2,1,16,128]{3,1,0,2:T(1,128)S(1)}, f32[2,1,16,128]{3,1,0,2:T(1,128)S(1)}, u32[]{:S(2)}, u32[]{:S(2)}) %collective-permute-start.8) | collective-permute-done | bytes 16416 | tf_op jit(solution)/shard_map/ppermute | solution.py:20
  43.7 0.3 fusion.40
  44.0 8.4 %all_to_all.72 = f32[2,16,16,128]{3,1,0,2:T(8,128)S(1)} all-to-all(f32[2,16,16,128]{3,1,0,2:T(8,128)S(1)} %fusion.40), channel_id=1, replica_groups=mesh['img'=4,'gx'=2,'gz'=4] {'gz'}, dimensions={2} | all-to-all | bytes 524288 | tf_op jit(solution)/shard_map/all_to_all | solution.py:60
  52.5 0.2 copy.99
  52.6 0.1 all_to_all.59
  52.7 2.1 %fusion.4 = f32[2,16,4,512]{3,1,2,0:T(8,128)S(1)} fusion(f32[2,16,4,512]{3,1,2,0:T(8,128)S(1)} %all_to_all.59, f32[2,512,512]{2,1,0:T(8,128)S(1)} %copy-done), kind=kOutput, calls=%fused_computation.4 | convolution fusion | flops 402653184 | bytes 2621440 | tf_op jit(solution)/shard_map/sij,sabj->sabi/dot_general | solution.py:57
  55.0 0.4 collective-permute-start.10
  55.4 1.4 %collective-permute-start.11 = (f32[2,16,4,128]{3,1,2,0:T(8,128)S(1)}, f32[2,16,4,128]{3,1,2,0:T(8,128)S(1)}, u32[]{:S(2)}, u32[]{:S(2)}) collective-permute-start(f32[2,16,4,128]{3,1,2,0:T(8,128)S(1)} %get-tuple-element.24), channel_id=1, source_target_pairs={{0,3},{1,2},{2,1},{3,0},{4,7},{5,6},{6,5},{7,4},{8,11},{9,10},{10,... | collective-permute-start | bytes 196616 | tf_op jit(solution)/shard_map/ppermute | solution.py:73
  56.9 3.0 %collective-permute-done.10 = f32[2,16,4,128]{3,1,2,0:T(8,128)S(1)} collective-permute-done((f32[2,16,4,128]{3,1,2,0:T(8,128)S(1)}, f32[2,16,4,128]{3,1,2,0:T(8,128)S(1)}, u32[]{:S(2)}, u32[]{:S(2)}) %collective-permute-start.10) | collective-permute-done | bytes 65568 | tf_op jit(solution)/shard_map/ppermute | solution.py:73
  60.0 0.5 collective-permute-done.11
  60.5 1.6 %collective-permute-start.12 = (f32[2,1,16,128]{3,1,0,2:T(1,128)S(1)}, f32[2,1,16,128]{3,1,0,2:T(1,128)S(1)}, u32[]{:S(2)}, u32[]{:S(2)}) collective-permute-start(f32[2,1,16,128]{3,1,0,2:T(1,128)S(1)} %get-tuple-element.22), channel_id=1, source_target_pairs={{0,4},{1,5},{2,6},{3,7},{8,12},{9,13},{10,14},{11,15},{16,20},{17,... | collective-permute-start | bytes 49160 | tf_op jit(solution)/shard_map/ppermute | solution.py:18
  62.2 1.3 collective-permute-start.13
  63.6 4.2 %collective-permute-done.13 = f32[2,1,16,128]{3,1,0,2:T(1,128)S(1)} collective-permute-done((f32[2,1,16,128]{3,1,0,2:T(1,128)S(1)}, f32[2,1,16,128]{3,1,0,2:T(1,128)S(1)}, u32[]{:S(2)}, u32[]{:S(2)}) %collective-permute-start.13) | collective-permute-done | bytes 16416 | tf_op jit(solution)/shard_map/ppermute | solution.py:20
  67.9 0.3 fusion.27
  68.2 8.4 %all_to_all.73 = f32[2,16,16,128]{3,1,0,2:T(8,128)S(1)} all-to-all(f32[2,16,16,128]{3,1,0,2:T(8,128)S(1)} %fusion.27), channel_id=1, replica_groups=mesh['img'=4,'gx'=2,'gz'=4] {'gz'}, dimensions={2} | all-to-all | bytes 524288 | tf_op jit(solution)/shard_map/all_to_all | solution.py:60
  76.6 0.2 copy.98
  76.8 0.1 all_to_all.63
  76.9 2.1 %fusion.2 = f32[2,16,4,512]{3,1,2,0:T(8,128)S(1)} fusion(f32[2,16,4,512]{3,1,2,0:T(8,128)S(1)} %all_to_all.63, f32[2,512,512]{2,1,0:T(8,128)S(1)} %copy-done), kind=kOutput, calls=%fused_computation.2 | convolution fusion | flops 402653184 | bytes 2621440 | tf_op jit(solution)/shard_map/sij,sabj->sabi/dot_general | solution.py:57
  79.2 0.4 collective-permute-start.15
  79.6 1.4 %collective-permute-start.16 = (f32[2,16,4,128]{3,1,2,0:T(8,128)S(1)}, f32[2,16,4,128]{3,1,2,0:T(8,128)S(1)}, u32[]{:S(2)}, u32[]{:S(2)}) collective-permute-start(f32[2,16,4,128]{3,1,2,0:T(8,128)S(1)} %get-tuple-element.16), channel_id=1, source_target_pairs={{0,3},{1,2},{2,1},{3,0},{4,7},{5,6},{6,5},{7,4},{8,11},{9,10},{10,... | collective-permute-start | bytes 196616 | tf_op jit(solution)/shard_map/ppermute | solution.py:73
  81.1 3.0 %collective-permute-done.15 = f32[2,16,4,128]{3,1,2,0:T(8,128)S(1)} collective-permute-done((f32[2,16,4,128]{3,1,2,0:T(8,128)S(1)}, f32[2,16,4,128]{3,1,2,0:T(8,128)S(1)}, u32[]{:S(2)}, u32[]{:S(2)}) %collective-permute-start.15) | collective-permute-done | bytes 65568 | tf_op jit(solution)/shard_map/ppermute | solution.py:73
  84.1 0.5 collective-permute-done.16
  84.7 1.6 %collective-permute-start.17 = (f32[2,1,16,128]{3,1,0,2:T(1,128)S(1)}, f32[2,1,16,128]{3,1,0,2:T(1,128)S(1)}, u32[]{:S(2)}, u32[]{:S(2)}) collective-permute-start(f32[2,1,16,128]{3,1,0,2:T(1,128)S(1)} %get-tuple-element.14), channel_id=1, source_target_pairs={{0,4},{1,5},{2,6},{3,7},{8,12},{9,13},{10,14},{11,15},{16,20},{17,... | collective-permute-start | bytes 49160 | tf_op jit(solution)/shard_map/ppermute | solution.py:18
  86.3 1.3 collective-permute-start.18
  87.7 4.2 %collective-permute-done.18 = f32[2,1,16,128]{3,1,0,2:T(1,128)S(1)} collective-permute-done((f32[2,1,16,128]{3,1,0,2:T(1,128)S(1)}, f32[2,1,16,128]{3,1,0,2:T(1,128)S(1)}, u32[]{:S(2)}, u32[]{:S(2)}) %collective-permute-start.18) | collective-permute-done | bytes 16416 | tf_op jit(solution)/shard_map/ppermute | solution.py:20
  92.0 1.0 fusion.14
  93.0 3.6 %all-to-all-start.3 = ((f32[2,16,16,128]{3,1,0,2:T(8,128)}), f32[2,16,16,128]{3,1,0,2:T(8,128)S(1)}, u32[]{:S(2)}, u32[]{:S(2)}) async-start(f32[2,16,16,128]{3,1,0,2:T(8,128)} %fusion.14), calls=%async_computation.3 | async-start | bytes 524288 | tf_op jit(solution)/shard_map/all_to_all | solution.py:60
  96.6 0.6 select_reduce_fusion.1
  97.3 5.2 %all-to-all-done.3 = f32[2,16,16,128]{3,1,0,2:T(8,128)S(1)} async-done(((f32[2,16,16,128]{3,1,0,2:T(8,128)}), f32[2,16,16,128]{3,1,0,2:T(8,128)S(1)}, u32[]{:S(2)}, u32[]{:S(2)}) %all-to-all-start.3) | async-done | bytes 262176 | tf_op jit(solution)/shard_map/all_to_all | solution.py:60
  102.4 0.2 copy.97
  102.6 0.1 all_to_all.67
  102.7 2.1 %fusion = f32[2,16,4,512]{3,1,2,0:T(8,128)S(1)} fusion(f32[2,16,4,512]{3,1,2,0:T(8,128)S(1)} %all_to_all.67, f32[2,512,512]{2,1,0:T(8,128)S(1)} %copy-done), kind=kOutput, calls=%fused_computation | convolution fusion | flops 402653184 | bytes 2621440 | tf_op jit(solution)/shard_map/sij,sabj->sabi/dot_general | solution.py:57
  105.0 0.4 collective-permute-start.20
  105.4 1.4 %collective-permute-start.21 = (f32[2,16,4,128]{3,1,2,0:T(8,128)S(1)}, f32[2,16,4,128]{3,1,2,0:T(8,128)S(1)}, u32[]{:S(2)}, u32[]{:S(2)}) collective-permute-start(f32[2,16,4,128]{3,1,2,0:T(8,128)S(1)} %get-tuple-element.8), channel_id=1, source_target_pairs={{0,3},{1,2},{2,1},{3,0},{4,7},{5,6},{6,5},{7,4},{8,11},{9,10},{10,... | collective-permute-start | bytes 196616 | tf_op jit(solution)/shard_map/ppermute | solution.py:73
  106.9 3.0 %collective-permute-done.20 = f32[2,16,4,128]{3,1,2,0:T(8,128)S(1)} collective-permute-done((f32[2,16,4,128]{3,1,2,0:T(8,128)S(1)}, f32[2,16,4,128]{3,1,2,0:T(8,128)S(1)}, u32[]{:S(2)}, u32[]{:S(2)}) %collective-permute-start.20) | collective-permute-done | bytes 65568 | tf_op jit(solution)/shard_map/ppermute | solution.py:73
  110.0 0.5 collective-permute-done.21
  110.5 1.3 collective-permute-start.22
  111.8 1.3 collective-permute-start.23
  113.1 4.6 %collective-permute-start.24 = (f32[2,16,16,128]{3,1,0,2:T(8,128)S(1)}, f32[2,16,16,128]{3,1,0,2:T(8,128)S(1)}, u32[]{:S(2)}, u32[]{:S(2)}) collective-permute-start(f32[2,16,16,128]{3,1,0,2:T(8,128)S(1)} %copy_dynamic-update-slice_fusion), channel_id=1, source_target_pairs={{8,0},{16,8},{24,16},{9,1},{17,9},{25,17},{10,2},{18,10},{26,18},{... | collective-permute-start | bytes 786440 | tf_op jit(solution)/shard_map/ppermute | solution.py:30
  117.6 5.5 %collective-permute-start.25 = (f32[2,16,16,128]{3,1,0,2:T(8,128)S(1)}, f32[2,16,16,128]{3,1,0,2:T(8,128)S(1)}, u32[]{:S(2)}, u32[]{:S(2)}) collective-permute-start(f32[2,16,16,128]{3,1,0,2:T(8,128)S(1)} %copy_dynamic-update-slice_fusion), channel_id=1, source_target_pairs={{16,0},{24,8},{17,1},{25,9},{18,2},{26,10},{19,3},{27,11},{20,4},{... | collective-permute-start | bytes 786440 | tf_op jit(solution)/shard_map/ppermute | solution.py:30
  128.2 0.7 fusion.77
  141.3 0.1 add_bitcast_fusion
  141.5 0.9 copy.58
  (67 shorter events, 1.7 us)
Async XLA Ops:
  0.0 27.9 %copy-start = (f32[2,512,512]{2,1,0:T(8,128)S(1)}, f32[2,512,512]{2,1,0:T(8,128)}, u32[]{:S(2)}) copy-start(f32[2,512,512]{2,1,0:T(8,128)} %param.7) | copy-start | bytes 6291460
  0.0 17.1 %copy-start.1 = (f32[2,16,16,128]{3,2,1,0:T(8,128)S(1)}, f32[2,16,16,128]{3,2,1,0:T(8,128)}, u32[]{:S(2)}) copy-start(f32[2,16,16,128]{3,2,1,0:T(8,128)} %param.6) | copy-start | bytes 786436
  0.9 16.1 %collective-permute-start = (f32[2,1,16,128]{3,1,0,2:T(1,128)S(1)}, f32[2,1,16,128]{3,1,0,2:T(1,128)S(1)}, u32[]{:S(2)}, u32[]{:S(2)}) collective-permute-start(f32[2,1,16,128]{3,1,0,2:T(1,128)S(1)} %copy.29), channel_id=1, source_target_pairs={{0,4},{1,5},{2,6},{3,7},{8,12},{9,13},{10,14},{11,15},{16,20},{17,... | collective-permute-start | bytes 49160 | tf_op jit(solution)/shard_map/ppermute | solution.py:18
  4.4 12.6 %collective-permute-start.2 = (f32[2,1,16,128]{3,1,0,2:T(1,128)S(1)}, f32[2,1,16,128]{3,1,0,2:T(1,128)S(1)}, u32[]{:S(2)}, u32[]{:S(2)}) collective-permute-start(f32[2,1,16,128]{3,1,0,2:T(1,128)S(1)} %copy.32), channel_id=1, source_target_pairs={{4,0},{5,1},{6,2},{7,3},{12,8},{13,9},{14,10},{15,11},{20,16},{21,... | collective-permute-start | bytes 49160 | tf_op jit(solution)/shard_map/ppermute | solution.py:20
  6.7 8.0 %collective-permute-start.1 = (f32[2,1,16,128]{3,1,0,2:T(1,128)S(1)}, f32[2,1,16,128]{3,1,0,2:T(1,128)S(1)}, u32[]{:S(2)}, u32[]{:S(2)}) collective-permute-start(f32[2,1,16,128]{3,1,0,2:T(1,128)S(1)} %get-tuple-element.42), channel_id=1, source_target_pairs={{0,4},{1,5},{2,6},{3,7},{8,12},{9,13},{10,14},{11,15},{16,20},{17,... | collective-permute-start | bytes 49160 | tf_op jit(solution)/shard_map/ppermute | solution.py:18
  11.3 5.6 %collective-permute-start.3 = (f32[2,1,16,128]{3,1,0,2:T(1,128)S(1)}, f32[2,1,16,128]{3,1,0,2:T(1,128)S(1)}, u32[]{:S(2)}, u32[]{:S(2)}) collective-permute-start(f32[2,1,16,128]{3,1,0,2:T(1,128)S(1)} %get-tuple-element.43), channel_id=1, source_target_pairs={{4,0},{5,1},{6,2},{7,3},{12,8},{13,9},{14,10},{15,11},{20,16},{21,... | collective-permute-start | bytes 49160 | tf_op jit(solution)/shard_map/ppermute | solution.py:20
  18.2 9.4 %all-to-all-start = ((f32[2,16,16,128]{3,1,0,2:T(8,128)}), f32[2,16,16,128]{3,1,0,2:T(8,128)S(1)}, u32[]{:S(2)}, u32[]{:S(2)}) async-start(f32[2,16,16,128]{3,1,0,2:T(8,128)} %get-tuple-element.5), calls=%async_computation | async-start | bytes 524288 | tf_op jit(solution)/shard_map/all_to_all | solution.py:60
  30.1 2.0 %collective-permute-start.4 = (f32[2,16,4,128]{3,1,2,0:T(8,128)S(1)}, f32[2,16,4,128]{3,1,2,0:T(8,128)S(1)}, u32[]{:S(2)}, u32[]{:S(2)}) collective-permute-start(f32[2,16,4,128]{3,1,2,0:T(8,128)S(1)} %get-tuple-element.34), channel_id=1, source_target_pairs={{0,1},{1,0},{2,3},{3,2},{4,5},{5,4},{6,7},{7,6},{8,9},{9,8},{10,11... | collective-permute-start | bytes 196616 | tf_op jit(solution)/shard_map/ppermute | solution.py:73
  30.1 5.0 %collective-permute-start.5 = (f32[2,16,4,128]{3,1,2,0:T(8,128)S(1)}, f32[2,16,4,128]{3,1,2,0:T(8,128)S(1)}, u32[]{:S(2)}, u32[]{:S(2)}) collective-permute-start(f32[2,16,4,128]{3,1,2,0:T(8,128)S(1)} %get-tuple-element.33), channel_id=1, source_target_pairs={{0,2},{1,3},{2,0},{3,1},{4,6},{5,7},{6,4},{7,5},{8,10},{9,11},{10,... | collective-permute-start | bytes 196616 | tf_op jit(solution)/shard_map/ppermute | solution.py:73
  30.6 5.0 %collective-permute-start.6 = (f32[2,16,4,128]{3,1,2,0:T(8,128)S(1)}, f32[2,16,4,128]{3,1,2,0:T(8,128)S(1)}, u32[]{:S(2)}, u32[]{:S(2)}) collective-permute-start(f32[2,16,4,128]{3,1,2,0:T(8,128)S(1)} %get-tuple-element.32), channel_id=1, source_target_pairs={{0,3},{1,2},{2,1},{3,0},{4,7},{5,6},{6,5},{7,4},{8,11},{9,10},{10,... | collective-permute-start | bytes 196616 | tf_op jit(solution)/shard_map/ppermute | solution.py:73
  35.6 3.8 %collective-permute-start.7 = (f32[2,1,16,128]{3,1,0,2:T(1,128)S(1)}, f32[2,1,16,128]{3,1,0,2:T(1,128)S(1)}, u32[]{:S(2)}, u32[]{:S(2)}) collective-permute-start(f32[2,1,16,128]{3,1,0,2:T(1,128)S(1)} %get-tuple-element.30), channel_id=1, source_target_pairs={{0,4},{1,5},{2,6},{3,7},{8,12},{9,13},{10,14},{11,15},{16,20},{17,... | collective-permute-start | bytes 49160 | tf_op jit(solution)/shard_map/ppermute | solution.py:18
  38.0 5.6 %collective-permute-start.8 = (f32[2,1,16,128]{3,1,0,2:T(1,128)S(1)}, f32[2,1,16,128]{3,1,0,2:T(1,128)S(1)}, u32[]{:S(2)}, u32[]{:S(2)}) collective-permute-start(f32[2,1,16,128]{3,1,0,2:T(1,128)S(1)} %get-tuple-element.31), channel_id=1, source_target_pairs={{4,0},{5,1},{6,2},{7,3},{12,8},{13,9},{14,10},{15,11},{20,16},{21,... | collective-permute-start | bytes 49160 | tf_op jit(solution)/shard_map/ppermute | solution.py:20
  54.9 2.0 %collective-permute-start.9 = (f32[2,16,4,128]{3,1,2,0:T(8,128)S(1)}, f32[2,16,4,128]{3,1,2,0:T(8,128)S(1)}, u32[]{:S(2)}, u32[]{:S(2)}) collective-permute-start(f32[2,16,4,128]{3,1,2,0:T(8,128)S(1)} %get-tuple-element.26), channel_id=1, source_target_pairs={{0,1},{1,0},{2,3},{3,2},{4,5},{5,4},{6,7},{7,6},{8,9},{9,8},{10,11... | collective-permute-start | bytes 196616 | tf_op jit(solution)/shard_map/ppermute | solution.py:73
  55.0 5.0 %collective-permute-start.10 = (f32[2,16,4,128]{3,1,2,0:T(8,128)S(1)}, f32[2,16,4,128]{3,1,2,0:T(8,128)S(1)}, u32[]{:S(2)}, u32[]{:S(2)}) collective-permute-start(f32[2,16,4,128]{3,1,2,0:T(8,128)S(1)} %get-tuple-element.25), channel_id=1, source_target_pairs={{0,2},{1,3},{2,0},{3,1},{4,6},{5,7},{6,4},{7,5},{8,10},{9,11},{10,... | collective-permute-start | bytes 196616 | tf_op jit(solution)/shard_map/ppermute | solution.py:73
  55.4 5.0 %collective-permute-start.11 = (f32[2,16,4,128]{3,1,2,0:T(8,128)S(1)}, f32[2,16,4,128]{3,1,2,0:T(8,128)S(1)}, u32[]{:S(2)}, u32[]{:S(2)}) collective-permute-start(f32[2,16,4,128]{3,1,2,0:T(8,128)S(1)} %get-tuple-element.24), channel_id=1, source_target_pairs={{0,3},{1,2},{2,1},{3,0},{4,7},{5,6},{6,5},{7,4},{8,11},{9,10},{10,... | collective-permute-start | bytes 196616 | tf_op jit(solution)/shard_map/ppermute | solution.py:73
  60.5 3.1 %collective-permute-start.12 = (f32[2,1,16,128]{3,1,0,2:T(1,128)S(1)}, f32[2,1,16,128]{3,1,0,2:T(1,128)S(1)}, u32[]{:S(2)}, u32[]{:S(2)}) collective-permute-start(f32[2,1,16,128]{3,1,0,2:T(1,128)S(1)} %get-tuple-element.22), channel_id=1, source_target_pairs={{0,4},{1,5},{2,6},{3,7},{8,12},{9,13},{10,14},{11,15},{16,20},{17,... | collective-permute-start | bytes 49160 | tf_op jit(solution)/shard_map/ppermute | solution.py:18
  62.2 5.6 %collective-permute-start.13 = (f32[2,1,16,128]{3,1,0,2:T(1,128)S(1)}, f32[2,1,16,128]{3,1,0,2:T(1,128)S(1)}, u32[]{:S(2)}, u32[]{:S(2)}) collective-permute-start(f32[2,1,16,128]{3,1,0,2:T(1,128)S(1)} %get-tuple-element.23), channel_id=1, source_target_pairs={{4,0},{5,1},{6,2},{7,3},{12,8},{13,9},{14,10},{15,11},{20,16},{21,... | collective-permute-start | bytes 49160 | tf_op jit(solution)/shard_map/ppermute | solution.py:20
  79.1 2.0 %collective-permute-start.14 = (f32[2,16,4,128]{3,1,2,0:T(8,128)S(1)}, f32[2,16,4,128]{3,1,2,0:T(8,128)S(1)}, u32[]{:S(2)}, u32[]{:S(2)}) collective-permute-start(f32[2,16,4,128]{3,1,2,0:T(8,128)S(1)} %get-tuple-element.18), channel_id=1, source_target_pairs={{0,1},{1,0},{2,3},{3,2},{4,5},{5,4},{6,7},{7,6},{8,9},{9,8},{10,11... | collective-permute-start | bytes 196616 | tf_op jit(solution)/shard_map/ppermute | solution.py:73
  79.2 5.0 %collective-permute-start.15 = (f32[2,16,4,128]{3,1,2,0:T(8,128)S(1)}, f32[2,16,4,128]{3,1,2,0:T(8,128)S(1)}, u32[]{:S(2)}, u32[]{:S(2)}) collective-permute-start(f32[2,16,4,128]{3,1,2,0:T(8,128)S(1)} %get-tuple-element.17), channel_id=1, source_target_pairs={{0,2},{1,3},{2,0},{3,1},{4,6},{5,7},{6,4},{7,5},{8,10},{9,11},{10,... | collective-permute-start | bytes 196616 | tf_op jit(solution)/shard_map/ppermute | solution.py:73
  79.6 5.0 %collective-permute-start.16 = (f32[2,16,4,128]{3,1,2,0:T(8,128)S(1)}, f32[2,16,4,128]{3,1,2,0:T(8,128)S(1)}, u32[]{:S(2)}, u32[]{:S(2)}) collective-permute-start(f32[2,16,4,128]{3,1,2,0:T(8,128)S(1)} %get-tuple-element.16), channel_id=1, source_target_pairs={{0,3},{1,2},{2,1},{3,0},{4,7},{5,6},{6,5},{7,4},{8,11},{9,10},{10,... | collective-permute-start | bytes 196616 | tf_op jit(solution)/shard_map/ppermute | solution.py:73
  84.1 12.5 %copy-start.3 = (s32[4]{0:T(128)S(1)}, s32[4]{0:T(128)}, u32[]{:S(2)}) copy-start(s32[4]{0:T(128)} %param.8) | copy-start | bytes 52
  84.7 3.1 %collective-permute-start.17 = (f32[2,1,16,128]{3,1,0,2:T(1,128)S(1)}, f32[2,1,16,128]{3,1,0,2:T(1,128)S(1)}, u32[]{:S(2)}, u32[]{:S(2)}) collective-permute-start(f32[2,1,16,128]{3,1,0,2:T(1,128)S(1)} %get-tuple-element.14), channel_id=1, source_target_pairs={{0,4},{1,5},{2,6},{3,7},{8,12},{9,13},{10,14},{11,15},{16,20},{17,... | collective-permute-start | bytes 49160 | tf_op jit(solution)/shard_map/ppermute | solution.py:18
  86.3 5.6 %collective-permute-start.18 = (f32[2,1,16,128]{3,1,0,2:T(1,128)S(1)}, f32[2,1,16,128]{3,1,0,2:T(1,128)S(1)}, u32[]{:S(2)}, u32[]{:S(2)}) collective-permute-start(f32[2,1,16,128]{3,1,0,2:T(1,128)S(1)} %get-tuple-element.15), channel_id=1, source_target_pairs={{4,0},{5,1},{6,2},{7,3},{12,8},{13,9},{14,10},{15,11},{20,16},{21,... | collective-permute-start | bytes 49160 | tf_op jit(solution)/shard_map/ppermute | solution.py:20
  93.0 9.4 %all-to-all-start.3 = ((f32[2,16,16,128]{3,1,0,2:T(8,128)}), f32[2,16,16,128]{3,1,0,2:T(8,128)S(1)}, u32[]{:S(2)}, u32[]{:S(2)}) async-start(f32[2,16,16,128]{3,1,0,2:T(8,128)} %fusion.14), calls=%async_computation.3 | async-start | bytes 524288 | tf_op jit(solution)/shard_map/all_to_all | solution.py:60
  102.7 25.4 %copy-start.2 = (f32[4,4]{1,0:T(4,128)S(1)}, f32[4,4]{1,0:T(4,128)}, u32[]{:S(2)}) copy-start(f32[4,4]{1,0:T(4,128)} %param.9) | copy-start | bytes 196
  104.9 2.0 %collective-permute-start.19 = (f32[2,16,4,128]{3,1,2,0:T(8,128)S(1)}, f32[2,16,4,128]{3,1,2,0:T(8,128)S(1)}, u32[]{:S(2)}, u32[]{:S(2)}) collective-permute-start(f32[2,16,4,128]{3,1,2,0:T(8,128)S(1)} %get-tuple-element.10), channel_id=1, source_target_pairs={{0,1},{1,0},{2,3},{3,2},{4,5},{5,4},{6,7},{7,6},{8,9},{9,8},{10,11... | collective-permute-start | bytes 196616 | tf_op jit(solution)/shard_map/ppermute | solution.py:73
  105.0 5.0 %collective-permute-start.20 = (f32[2,16,4,128]{3,1,2,0:T(8,128)S(1)}, f32[2,16,4,128]{3,1,2,0:T(8,128)S(1)}, u32[]{:S(2)}, u32[]{:S(2)}) collective-permute-start(f32[2,16,4,128]{3,1,2,0:T(8,128)S(1)} %get-tuple-element.9), channel_id=1, source_target_pairs={{0,2},{1,3},{2,0},{3,1},{4,6},{5,7},{6,4},{7,5},{8,10},{9,11},{10,... | collective-permute-start | bytes 196616 | tf_op jit(solution)/shard_map/ppermute | solution.py:73
  105.4 5.0 %collective-permute-start.21 = (f32[2,16,4,128]{3,1,2,0:T(8,128)S(1)}, f32[2,16,4,128]{3,1,2,0:T(8,128)S(1)}, u32[]{:S(2)}, u32[]{:S(2)}) collective-permute-start(f32[2,16,4,128]{3,1,2,0:T(8,128)S(1)} %get-tuple-element.8), channel_id=1, source_target_pairs={{0,3},{1,2},{2,1},{3,0},{4,7},{5,6},{6,5},{7,4},{8,11},{9,10},{10,... | collective-permute-start | bytes 196616 | tf_op jit(solution)/shard_map/ppermute | solution.py:73
  110.5 30.8 %collective-permute-start.22 = (f32[2,16,16,128]{3,1,0,2:T(8,128)S(1)}, f32[2,16,16,128]{3,1,0,2:T(8,128)S(1)}, u32[]{:S(2)}, u32[]{:S(2)}) collective-permute-start(f32[2,16,16,128]{3,1,0,2:T(8,128)S(1)} %copy_dynamic-update-slice_fusion), channel_id=1, source_target_pairs={{0,16},{8,24},{1,17},{9,25},{2,18},{10,26},{3,19},{11,27},{4,20},{... | collective-permute-start | bytes 786440 | tf_op jit(solution)/shard_map/ppermute | solution.py:30
  111.8 29.5 %collective-permute-start.23 = (f32[2,16,16,128]{3,1,0,2:T(8,128)S(1)}, f32[2,16,16,128]{3,1,0,2:T(8,128)S(1)}, u32[]{:S(2)}, u32[]{:S(2)}) collective-permute-start(f32[2,16,16,128]{3,1,0,2:T(8,128)S(1)} %copy_dynamic-update-slice_fusion), channel_id=1, source_target_pairs={{0,8},{8,16},{16,24},{1,9},{9,17},{17,25},{2,10},{10,18},{18,26},{... | collective-permute-start | bytes 786440 | tf_op jit(solution)/shard_map/ppermute | solution.py:30
  113.1 28.2 %collective-permute-start.24 = (f32[2,16,16,128]{3,1,0,2:T(8,128)S(1)}, f32[2,16,16,128]{3,1,0,2:T(8,128)S(1)}, u32[]{:S(2)}, u32[]{:S(2)}) collective-permute-start(f32[2,16,16,128]{3,1,0,2:T(8,128)S(1)} %copy_dynamic-update-slice_fusion), channel_id=1, source_target_pairs={{8,0},{16,8},{24,16},{9,1},{17,9},{25,17},{10,2},{18,10},{26,18},{... | collective-permute-start | bytes 786440 | tf_op jit(solution)/shard_map/ppermute | solution.py:30
  117.6 23.7 %collective-permute-start.25 = (f32[2,16,16,128]{3,1,0,2:T(8,128)S(1)}, f32[2,16,16,128]{3,1,0,2:T(8,128)S(1)}, u32[]{:S(2)}, u32[]{:S(2)}) collective-permute-start(f32[2,16,16,128]{3,1,0,2:T(8,128)S(1)} %copy_dynamic-update-slice_fusion), channel_id=1, source_target_pairs={{16,0},{24,8},{17,1},{25,9},{18,2},{26,10},{19,3},{27,11},{20,4},{... | collective-permute-start | bytes 786440 | tf_op jit(solution)/shard_map/ppermute | solution.py:30
